TPU v7x, 512 devices: a whole 4x8x8 slice. The times are simulated.
512 devices in a mesh: attn: 32 (over x, z_lo, core), grp: 2 (over z_hi), tp: 8 (over y).
Axes of the slice: x: 4, y: 8, z: 8 (z_hi: 2, z_lo: 4; z = z_hi * 4 + z_lo), core: 2. Of those that a mesh axis runs over, the one named last changes fastest.
Arguments:
- queries: bfloat16 [1536, 6144], P(('attn', 'grp'), 'tp'), may hold values from -33 to 33
- new_keys: bfloat16 [1536, 1024], P(('attn', 'grp'), 'tp'), may hold values from -6 to 6
- new_values: bfloat16 [1536, 1024], P(('attn', 'grp'), 'tp'), may hold values from -6 to 6
- key_pages: bfloat16 [15360, 16, 1024], P(('attn', 'grp'), None, 'tp'), may hold values from -13 to 13
- value_pages: bfloat16 [15360, 16, 1024], P(('attn', 'grp'), None, 'tp'), may hold values from -6 to 6
- page_order: int32 [64, 240], P(('attn', 'grp')), may hold values from 0 to 239, each once within a row
- page_counts: int32 [64, 24], P(('attn', 'grp')), may hold values from 1 to 32, 240 in all within a row
- residual: bfloat16 [1536, 6144], P(('attn', 'grp'), 'tp'), may hold values from -3 to 3
- norm_gain: float32 [6144], P('tp'), may hold values from 0.1 to 1.9
- routes: int32 [1536, 2], P(('attn', 'grp')), may hold values from 0 to 7, all different within a row; in each aligned block of 24 rows (0 to 23, 24 to 47, ...) at most 12 rows name the same one
- route_weights: float32 [1536, 2], P(('attn', 'grp')), may hold values from 0.1 to 0.9
- w_gate: bfloat16 [2, 6144, 16384], P('grp', 'tp', 'attn'), may hold values from -0.078125 to 0.078125
- w_up: bfloat16 [2, 6144, 16384], P('grp', 'tp', 'attn'), may hold values from -0.078125 to 0.078125
- w_down: bfloat16 [2, 16384, 6144], P('grp', 'attn', 'tp'), may hold values from -0.046875 to 0.046875
Outputs:
- layer_out: bfloat16 [1536, 6144], P(('attn', 'grp'), 'tp')
Inputs may be any that keep to these rules, and one draw needn't show every extreme that they name: `routes`: within one block of 24 rows the two experts of a row differ, and no expert is named by more than 12 rows of the block. Each row's page_order is a permutation of 0 to 239. `page_counts`: each block's counts sum to 240.
All inputs are finite; a program needn't handle non-finite values.
Results may differ from a plain program's by a relative error of at most 0.015.
Values may be sent and summed in bfloat16 or wider, within the bound.
A program may use at most 64 MiB of HBM per device.

v0:
```python
import math

import jax
import jax.numpy as jnp
from jax import lax
from jax.sharding import PartitionSpec as P

D = 6144
HD = 128
PAGE = 16
MAXP = 32
ROWS_DEV = 24


norm_epsilon = 1e-05


def attend(query, new_key, new_value, key_pages, value_pages, order, counts):
    count_rows = query.shape[0]
    kv_heads = new_key.shape[1] // HD
    group = query.shape[1] // new_key.shape[1]
    query_four = query.reshape(count_rows, kv_heads, group, HD)
    starts = jnp.cumsum(counts) - counts
    offsets = starts[:, None] + jnp.arange(MAXP, dtype=jnp.int32)[None, :]
    offsets = jnp.minimum(offsets, order.shape[0] - 1)
    pages = order[offsets]
    live = jnp.arange(MAXP, dtype=jnp.int32)[None, :] < counts[:, None]
    live = jnp.repeat(live, PAGE, axis=1)
    keys = key_pages[pages].reshape(count_rows, MAXP * PAGE, kv_heads, HD)
    values = value_pages[pages].reshape(count_rows, MAXP * PAGE, kv_heads, HD)
    scale = 1.0 / math.sqrt(HD)
    scores = (
        jnp.einsum("rkgd,rtkd->rkgt", query_four, keys, preferred_element_type=jnp.float32) * scale
    )
    scores = jnp.where(live[:, None, None, :], scores, -1e30)
    own_key = new_key.reshape(count_rows, kv_heads, HD)
    own = (
        jnp.einsum("rkgd,rkd->rkg", query_four, own_key, preferred_element_type=jnp.float32) * scale
    )
    top = jnp.maximum(jnp.max(scores, axis=3), own)
    weights = jnp.exp(scores - top[..., None])
    own_weight = jnp.exp(own - top)
    total = jnp.sum(weights, axis=3) + own_weight
    weights_low = weights.astype(jnp.bfloat16)
    own_low = own_weight.astype(jnp.bfloat16).astype(jnp.float32)
    own_value = new_value.astype(jnp.float32).reshape(count_rows, kv_heads, 1, HD)
    mixed = (
        jnp.einsum("rkgt,rtkd->rkgd", weights_low, values, preferred_element_type=jnp.float32)
        + own_low[..., None] * own_value
    )
    return (mixed / total[..., None]).reshape(count_rows, kv_heads * group * HD)


def local(
    queries,
    new_keys,
    new_values,
    key_pages,
    value_pages,
    page_order,
    page_counts,
    residual,
    norm_gain,
    routes,
    route_weights,
    w_gate,
    w_up,
    w_down,
):
    attention = attend(
        queries, new_keys, new_values, key_pages, value_pages, page_order[0], page_counts[0]
    )
    hidden = (residual.astype(jnp.float32) + attention).astype(jnp.bfloat16)
    hidden_wide = hidden.astype(jnp.float32)
    squares = lax.psum(jnp.sum(hidden_wide * hidden_wide, axis=1), "tp")
    normed = (hidden_wide * lax.rsqrt(squares / D + norm_epsilon)[:, None] * norm_gain).astype(
        jnp.bfloat16
    )
    experts = lax.axis_size("grp")
    cap = ROWS_DEV // 2
    width_block = normed.shape[1]
    onehot = routes[..., None] == jnp.arange(experts, dtype=jnp.int32)
    hits = jnp.any(onehot, axis=1).astype(jnp.int32)
    gating = jnp.sum(route_weights[..., None] * onehot.astype(jnp.float32), axis=1)
    position = jnp.cumsum(hits, axis=0) - hits
    chosen = (hits[..., None] == 1) & (position[..., None] == jnp.arange(cap, dtype=jnp.int32))
    chooser = jnp.transpose(chosen.astype(jnp.bfloat16), (1, 2, 0))
    outgoing = jnp.einsum(
        "ecr,rd->ecd", chooser, normed, preferred_element_type=jnp.float32
    ).astype(jnp.bfloat16)
    arrived = lax.all_to_all(outgoing, "grp", split_axis=0, concat_axis=0, tiled=True)
    slots_in = lax.all_gather(arrived, "attn", axis=0, tiled=True)
    slots_in = slots_in.reshape(-1, width_block)
    unit_block = w_gate.shape[2]
    joined = jnp.concatenate([w_gate[0], w_up[0]], axis=1)
    summed = lax.psum(
        jnp.dot(slots_in, joined, preferred_element_type=jnp.float32).astype(jnp.bfloat16), "tp"
    ).astype(jnp.float32)
    active = (jax.nn.silu(summed[:, :unit_block]) * summed[:, unit_block:]).astype(jnp.bfloat16)
    down_block = w_down[0]
    returned = lax.psum_scatter(
        jnp.dot(active, down_block, preferred_element_type=jnp.float32).astype(jnp.bfloat16),
        "attn",
        scatter_dimension=0,
        tiled=True,
    ).astype(jnp.float32)
    returned = returned.astype(jnp.bfloat16).reshape(experts, cap, width_block)
    home = lax.all_to_all(returned, "grp", split_axis=0, concat_axis=0, tiled=True)
    brought = jnp.einsum("ecr,ecd->red", chooser, home, preferred_element_type=jnp.float32)
    expert_sum = jnp.sum(gating[..., None] * brought, axis=1)
    return (hidden_wide + expert_sum).astype(jnp.bfloat16)


def solution(mesh):
    return jax.shard_map(
        local,
        mesh=mesh,
        in_specs=(
            P(("attn", "grp"), "tp"),
            P(("attn", "grp"), "tp"),
            P(("attn", "grp"), "tp"),
            P(("attn", "grp"), None, "tp"),
            P(("attn", "grp"), None, "tp"),
            P(("attn", "grp"), None),
            P(("attn", "grp"), None),
            P(("attn", "grp"), "tp"),
            P("tp"),
            P(("attn", "grp"), None),
            P(("attn", "grp"), None),
            P("grp", "tp", "attn"),
            P("grp", "tp", "attn"),
            P("grp", "attn", "tp"),
        ),
        out_specs=P(("attn", "grp"), "tp"),
        check_vma=False,
    )
```

profile of v0, /device:TPU:1, one launch (start us, length us, event | category | flops | bytes accessed | tf_op | source)
XLA Modules:
  0.0 381.5 jit_solution(2996315625945239237)
XLA Ops:
  6.5 0.8 copy.30
  7.4 0.1 reduce.4
  7.5 0.7 bitcast_subtract_fusion
  8.2 0.1 compare_select_fusion.1
  8.3 0.1 reshape.191
  8.4 0.0 copy-start.3
  8.4 5.0 %gather_fusion = s32[768]{0:T(1024)S(1)} fusion(s32[240]{0:T(256)S(1)} %bitcast.45, s32[1024]{0:T(1024)S(1)} %pad_clamp_fusion.1), kind=kCustom, calls=%fused_computation | custom fusion | bytes 9216 | tf_op jit(solution)/shard_map/gather | solution.py:26
  13.4 0.1 gather.12
  13.5 0.1 reshape.199
  13.5 0.1 reshape.184
  13.6 0.1 iota_compare_fusion.1
  13.7 0.2 broadcast_in_dim.16
  13.9 0.3 broadcast_in_dim.17
  14.1 0.0 copy-start.12
  14.2 3.5 gather_fusion.1
  17.7 0.1 fusion.27
  17.8 0.0 copy-start.2
  17.8 3.0 fusion.38
  20.8 0.2 fusion.11
  21.1 3.5 gather_fusion.2
  24.7 0.0 copy-start.6
  24.7 2.5 fusion.8
  27.2 0.1 fusion.15
  27.3 14.8 %psum.14 = f32[24]{0:T(128)S(1)} all-reduce(f32[24]{0:T(128)S(1)} %get-tuple-element.5), channel_id=1, replica_groups=mesh['attn'=32,'grp'=2,'tp'=8] {'tp'}, use_global_device_ids=true, to_apply=%region_7.8 | all-reduce | flops 24 | bytes 192 | tf_op jit(solution)/shard_map/psum | solution.py:75
  42.1 0.1 copy.31
  42.3 0.1 copy.33
  42.4 0.1 copy.32
  42.5 0.2 convolution_convert_fusion.2
  42.7 16.9 %all_to_all.10 = bf16[2,12,768]{2,1,0:T(8,128)(2,1)} all-to-all(bf16[2,12,768]{2,1,0:T(8,128)(2,1)S(1)} %convolution_convert_fusion.2), channel_id=1, replica_groups=mesh['attn'=32,'grp'=2,'tp'=8] {'grp'}, dimensions={0} | all-to-all | bytes 73728 | tf_op jit(solution)/shard_map/all_to_all | solution.py:91
  59.6 0.0 all-gather.2.cloned.1.call-update
  59.7 0.0 all-reduce.2.cloned.1.call-start
  59.7 64.3 %all-gather.2.cloned.1.call-done = bf16[64,12,768]{2,1,0:T(8,128)(2,1)} async-done(((bf16[2,12,768]{2,1,0:T(8,128)(2,1)}), bf16[64,12,768]{2,1,0:T(8,128)(2,1)}) %all-gather.2.cloned.1.call-update) | async-done | bytes 1179664 | tf_op jit(solution)/shard_map/all_gather | solution.py:92
  124.0 2.2 reshape.187
  126.3 3.7 convolution_convert_fusion
  130.0 0.0 all-reduce.2.cloned.1.call-update
  130.0 0.0 copy-start.11
  130.0 0.0 reduce-scatter.2.cloned.1.call-start
  130.1 78.7 %all-reduce.2.cloned.1.call-done = bf16[768,1024]{1,0:T(8,128)(2,1)} async-done(((bf16[768,1024]{1,0:T(8,128)(2,1)}), bf16[768,1024]{1,0:T(8,128)(2,1)}) %all-reduce.2.cloned.1.call-update) | async-done | bytes 1572880 | tf_op jit(solution)/shard_map/psum | solution.py:96
  208.8 1.8 convert_element_type.77
  210.6 0.0 copy-start.9
  210.6 2.0 convolution_convert_fusion.1
  212.6 0.0 reduce-scatter.2.cloned.1.call-update
  212.6 147.3 %reduce-scatter.2.cloned.1.call-done = bf16[24,768]{1,0:T(8,128)(2,1)} async-done(((bf16[768,768]{1,0:T(8,128)(2,1)}), bf16[24,768]{1,0:T(8,128)(2,1)}) %reduce-scatter.2.cloned.1.call-update) | async-done | bytes 36880 | tf_op jit(solution)/shard_map/reduce_scatter | solution.py:101
  360.0 1.4 reshape.188
  361.4 6.0 %all-to-all-start.1 = ((bf16[2,12,768]{2,1,0:T(8,128)(2,1)}), bf16[2,12,768]{2,1,0:T(8,128)(2,1)S(1)}, u32[]{:S(2)}, u32[]{:S(2)}) async-start(bf16[2,12,768]{2,1,0:T(8,128)(2,1)} %reshape.188), calls=%async_computation.2 | async-start | bytes 98304 | tf_op jit(solution)/shard_map/all_to_all | solution.py:108
  367.4 6.8 %all-to-all-done.1 = bf16[2,12,768]{2,1,0:T(8,128)(2,1)S(1)} async-done(((bf16[2,12,768]{2,1,0:T(8,128)(2,1)}), bf16[2,12,768]{2,1,0:T(8,128)(2,1)S(1)}, u32[]{:S(2)}, u32[]{:S(2)}) %all-to-all-start.1) | async-done | bytes 36896 | tf_op jit(solution)/shard_map/all_to_all | solution.py:108
  374.1 0.2 fusion.7
  374.3 0.6 fusion.18
  (34 shorter events, 0.2 us)
Async XLA Ops:
  6.5 7.6 %copy-start = (bf16[240,16,128]{2,1,0:T(8,128)(2,1)S(1)}, bf16[240,16,128]{2,1,0:T(8,128)(2,1)}, u32[]{:S(2)}) copy-start(bf16[240,16,128]{2,1,0:T(8,128)(2,1)} %param.17) | copy-start | bytes 2949124
  6.5 1.8 copy-start.1
  6.5 117.5 %all-gather.2.cloned.1.call-start = ((), (), s32[]{:S(2)}) async-start(), calls=%async_computation.3 | async-start | bytes 1622016 | tf_op jit(solution)/shard_map/all_gather | solution.py:92
  8.4 5.2 %copy-start.3 = (bf16[24,768]{1,0:T(8,128)(2,1)S(1)}, bf16[24,768]{1,0:T(8,128)(2,1)}, u32[]{:S(2)}) copy-start(bf16[24,768]{1,0:T(8,128)(2,1)} %param.14) | copy-start | bytes 110596
  8.4 5.2 %copy-start.7 = (s32[1,24]{1,0:T(1,128)S(1)}, s32[1,24]{1,0:T(1,128)}, u32[]{:S(2)}) copy-start(s32[1,24]{1,0:T(1,128)} %param.20) | copy-start | bytes 292
  14.1 3.5 copy-start.12
  17.8 3.2 copy-start.2
  21.1 3.5 copy-start.5
  24.6 2.5 copy-start.4
  24.6 17.5 %copy-start.8 = (s32[24,2]{0,1:T(2,128)S(1)}, s32[24,2]{0,1:T(2,128)}, u32[]{:S(2)}) copy-start(s32[24,2]{0,1:T(2,128)} %param.23) | copy-start | bytes 580
  24.7 17.8 %copy-start.6 = (f32[768]{0:T(1024)S(1)}, f32[768]{0:T(1024)}, u32[]{:S(2)}) copy-start(f32[768]{0:T(1024)} %param.22) | copy-start | bytes 9220
  27.3 99.0 %copy-start.10 = (bf16[1,768,512]{2,1,0:T(8,128)(2,1)S(1)}, bf16[1,768,512]{2,1,0:T(8,128)(2,1)}, u32[]{:S(2)}) copy-start(bf16[1,768,512]{2,1,0:T(8,128)(2,1)} %param.26) | copy-start | bytes 2359300
  59.7 149.1 %all-reduce.2.cloned.1.call-start = ((), (), s32[]{:S(2)}) async-start(), calls=%async_computation.4 | async-start | bytes 3145728 | tf_op jit(solution)/shard_map/psum | solution.py:96
  130.0 80.6 %copy-start.11 = (bf16[1,512,768]{2,1,0:T(8,128)(2,1)S(1)}, bf16[1,512,768]{2,1,0:T(8,128)(2,1)}, u32[]{:S(2)}) copy-start(bf16[1,512,768]{2,1,0:T(8,128)(2,1)} %param.27) | copy-start | bytes 2359300
  130.0 230.0 %reduce-scatter.2.cloned.1.call-start = ((), (), s32[]{:S(2)}) async-start(), calls=%async_computation.5 | async-start | bytes 1216512 | tf_op jit(solution)/shard_map/reduce_scatter | solution.py:101
  210.6 156.7 %copy-start.9 = (f32[24,2]{0,1:T(2,128)S(1)}, f32[24,2]{0,1:T(2,128)}, u32[]{:S(2)}) copy-start(f32[24,2]{0,1:T(2,128)} %param.24) | copy-start | bytes 580
  361.4 12.8 %all-to-all-start.1 = ((bf16[2,12,768]{2,1,0:T(8,128)(2,1)}), bf16[2,12,768]{2,1,0:T(8,128)(2,1)S(1)}, u32[]{:S(2)}, u32[]{:S(2)}) async-start(bf16[2,12,768]{2,1,0:T(8,128)(2,1)} %reshape.188), calls=%async_computation.2 | async-start | bytes 98304 | tf_op jit(solution)/shard_map/all_to_all | solution.py:108
Sparse Core Ops, SparseCore 0:
  59.8 64.2 all-gather.1
  130.1 78.6 all-reduce.1
  212.8 147.1 reduce-scatter.1
where the time goes:
time: 386 us; the launch traced here: 382 us
  waiting for transfers between devices  297 us (77%)
  blocking collectives  31.8 us (8%)
  local copies, waits for them, and re-layouts  17.6 us (5%)
  between operations  13.3 us (3%)
  matrix products  11.7 us (3%)
  starting transfers between devices  6.05 us (2%)
  other arithmetic  3.9 us (1%)
    reduce_scatter x1, waiting for transfers between devices, local(): lax.psum_scatter(jnp.dot(active, down_block, preferred_element_type=jnp.f...  147 us
    psum x1, waiting for transfers between devices, local(): lax.psum(jnp.dot(slots_in, joined, preferred_element_type=jnp.float32).as...  78.7 us
    all_gather x1, waiting for transfers between devices, local(): slots_in = lax.all_gather(arrived, 'attn', axis=0, tiled=True)  64.3 us
    all_to_all x1, blocking collectives, local(): lax.all_to_all(outgoing, 'grp', split_axis=0, concat_axis=0, tiled=True)  16.9 us
    psum x1, blocking collectives, local(): squares = lax.psum(jnp.sum(hidden_wide * hidden_wide, axis=1), 'tp')  14.8 us
  transfers between devices with their start and end apart: 4, of which 4 were waited for; matrix products, arithmetic and copies ran while one was open for 0% of the time, Pallas kernels for 0%

commit v1 on v0

v1 whole, which is shorter than its diff:
```python
import functools
import math

import jax
import jax.numpy as jnp
from jax import lax
from jax.experimental import pallas as pl
from jax.experimental.pallas import tpu as pltpu
from jax.sharding import PartitionSpec as P

HD = 128
PAGE = 16
CAP = 12
SLOT = 16
PADR = 32
NX = 4
NCORE = 2
NORM_EPSILON = 1e-05
MASKED = -1e30
MESH = pl.DeviceIdType.MESH
F32 = jnp.float32
BF16 = jnp.bfloat16


def iota(shape, dim):
    return lax.broadcasted_iota(jnp.int32, shape, dim)


def to_column(row, rows):
    n = row.shape[1]
    eye = iota((rows, n), 0) == iota((rows, n), 1)
    return jnp.sum(jnp.where(eye, row, jnp.zeros_like(row)), axis=1, keepdims=True)


def to_row(column, lanes):
    n = column.shape[0]
    eye = iota((n, lanes), 0) == iota((n, lanes), 1)
    return jnp.sum(jnp.where(eye, column, jnp.zeros_like(column)), axis=0, keepdims=True)


def before(column, lanes):
    n = column.shape[0]
    ahead = iota((n, lanes), 0) < iota((n, lanes), 1)
    return jnp.sum(jnp.where(ahead, column, jnp.zeros_like(column)), axis=0, keepdims=True)


def dot(a, b):
    return jnp.dot(a, b, preferred_element_type=F32)


def kernel(
    sizes,
    q_ref,
    nk_ref,
    nv_ref,
    order_ref,
    counts_ref,
    res_ref,
    gain_ref,
    routes_ref,
    rw_ref,
    k_hbm,
    v_hbm,
    wg_hbm,
    wu_hbm,
    wd_hbm,
    out_ref,
    kaug,
    vbuf,
    wg,
    wu,
    wd,
    scores,
    sq_own,
    sq_in,
    hid,
    outg,
    zin,
    xin,
    pre,
    rs_in,
    act,
    outp,
    core_in,
    ysum,
    half_in,
    full_in,
    zsend,
    zback,
    local_sems,
    send_sems,
    recv_sems,
):
    nattn, ngrp, nt, width_all = sizes
    rows, width = q_ref.shape
    heads = width // HD
    pool = order_ref.shape[1]
    nzl = nattn // (NX * NCORE)
    nz = nzl * ngrp
    hr = nz * CAP
    nb = nt // 2
    half = nt // 2
    hh = hr // 2

    a = lax.axis_index("attn")
    g = lax.axis_index("grp")
    t = lax.axis_index("tp")
    core = lax.rem(a, NCORE)
    zl = lax.rem(a // NCORE, nzl)
    x = a // (NCORE * nzl)
    z = g * nzl + zl

    def at_x(d):
        return {"attn": (lax.rem(x + d, NX) * nzl + zl) * NCORE + core, "grp": g, "tp": t}

    def at_z(d):
        to = lax.rem(z + d, nz)
        return {"attn": (x * nzl + lax.rem(to, nzl)) * NCORE + core, "grp": to // nzl, "tp": t}

    def at_t(d):
        return {"attn": a, "grp": g, "tp": lax.rem(t + d, nt)}

    sibling = {"attn": a + 1 - 2 * core, "grp": g, "tp": t}

    barrier = pltpu.get_barrier_semaphore()
    partners = [sibling, at_x(1), at_x(NX - 1)]
    partners += [at_z(d) for d in range(1, nz)]
    partners += [at_t(d) for d in range(1, nt)]
    for partner in partners:
        pl.semaphore_signal(barrier, inc=1, device_id=partner, device_id_type=MESH)

    loads = [
        pltpu.make_async_copy(k_hbm, kaug.at[:, :, pl.ds(0, HD)], local_sems.at[0]),
        pltpu.make_async_copy(v_hbm, vbuf, local_sems.at[1]),
        pltpu.make_async_copy(wg_hbm.at[0], wg, local_sems.at[2]),
        pltpu.make_async_copy(wu_hbm.at[0], wu, local_sems.at[3]),
        pltpu.make_async_copy(wd_hbm.at[0], wd, local_sems.at[4]),
    ]
    for load in loads:
        load.start()

    sent = []

    def push(src, dst, to):
        index = len(sent)
        copy = pltpu.make_async_remote_copy(
            src_ref=src,
            dst_ref=dst,
            send_sem=send_sems.at[index],
            recv_sem=recv_sems.at[index],
            device_id=to,
            device_id_type=MESH,
        )
        copy.start()
        sent.append(copy)
        return copy

    counts_col = to_column(counts_ref[...].astype(F32), rows)
    starts_row = before(counts_col, HD)
    counts_row = to_row(counts_col, HD)
    place = iota((pool, HD), 0).astype(F32)
    row_of_place = ((place >= starts_row) & (place < starts_row + counts_row)).astype(F32)
    place_of_page = (iota((pool, pool), 0) == order_ref[...]).astype(F32)
    owner = dot(place_of_page.astype(BF16), row_of_place.astype(BF16))
    kaug[:, :, pl.ds(HD, HD)] = jnp.broadcast_to(
        owner.reshape(pool, 1, HD), (pool, PAGE, HD)
    ).astype(BF16)
    own_row = iota((rows, HD), 0)
    lane = iota((rows, HD), 1)
    mask_block = jnp.where((own_row == lane) | (lane >= rows), 0.0, MASKED)

    q_wide = q_ref[...].astype(F32)
    q_rows = jnp.concatenate([q_wide[:, h * HD : (h + 1) * HD] for h in range(heads)], axis=0)
    q_aug = jnp.concatenate(
        [q_rows, jnp.concatenate([mask_block] * heads, axis=0)], axis=1
    ).astype(BF16)
    scale = 1.0 / math.sqrt(HD)
    new_key = jnp.concatenate([nk_ref[...].astype(F32)] * heads, axis=0)
    own = jnp.sum(q_rows * new_key, axis=1, keepdims=True) * scale

    loads[0].wait()
    pieces = scores.shape[0]
    pages = pool // pieces
    tokens = pages * PAGE

    def score_piece(i, top):
        keys = kaug[pl.ds(i * pages, pages)].reshape(tokens, 2 * HD)
        piece = (
            lax.dot_general(
                q_aug, keys, (((1,), (1,)), ((), ())), preferred_element_type=F32
            )
            * scale
        )
        scores[i] = piece
        return jnp.maximum(top, piece)

    top = lax.fori_loop(
        0, pieces, score_piece, jnp.full((heads * rows, tokens), MASKED, F32), unroll=True
    )
    top = jnp.maximum(jnp.max(top, axis=1, keepdims=True), own)
    own_weight = jnp.exp(own - top)

    loads[1].wait()

    def value_piece(i, carry):
        total, mixed = carry
        weights = jnp.exp(scores[i] - top)
        values = vbuf[pl.ds(i * pages, pages)].reshape(tokens, HD)
        return total + weights, mixed + dot(weights.astype(BF16), values)

    total, mixed = lax.fori_loop(
        0,
        pieces,
        value_piece,
        (jnp.zeros((heads * rows, tokens), F32), jnp.zeros((heads * rows, HD), F32)),
        unroll=True,
    )
    total = jnp.sum(total, axis=1, keepdims=True) + own_weight
    own_low = own_weight.astype(BF16).astype(F32)
    new_value = jnp.concatenate([nv_ref[...].astype(F32)] * heads, axis=0)
    attention = (mixed + own_low * new_value) / total
    attention = jnp.concatenate(
        [attention[h * rows : (h + 1) * rows] for h in range(heads)], axis=1
    )
    hidden = (res_ref[...].astype(F32) + attention).astype(BF16).astype(F32)
    hid[...] = hidden
    squares = jnp.sum(hidden * hidden, axis=1, keepdims=True)
    sq_own[...] = jnp.broadcast_to(to_row(squares, HD), sq_own.shape)

    routes = routes_ref[...]
    route_weights = rw_ref[...]
    chosen, gated = [], []
    for e in range(ngrp):
        named = routes == e
        hit_row = jnp.max(named.astype(F32), axis=0, keepdims=True)
        gate_row = jnp.sum(jnp.where(named, route_weights, 0.0), axis=0, keepdims=True)
        hit_col = to_column(hit_row, PADR)
        gate_col = to_column(gate_row, PADR)
        pos_row = before(hit_col, PADR)
        pos_col = to_column(pos_row, PADR)
        hit_wide = to_row(hit_col, PADR)
        slot = iota((SLOT, PADR), 0).astype(F32)
        chosen.append(jnp.where(slot == pos_row, hit_wide, 0.0))
        slot = iota((PADR, SLOT), 1).astype(F32)
        gated.append(jnp.where(slot == pos_col, hit_col * gate_col, 0.0))
    chooser = jnp.concatenate(chosen, axis=0).astype(BF16)
    gating = jnp.concatenate(gated, axis=1)

    pl.semaphore_wait(barrier, len(partners))

    copies = [push(sq_own, sq_in.at[d], at_t(d)) for d in range(1, nt)]
    for copy in copies:
        copy.wait_recv()
    total_row = sq_own[...]
    for d in range(1, nt):
        total_row = total_row + sq_in[d]
    squares = to_column(total_row[0:1, 0:rows], rows)
    normed = hid[...] * lax.rsqrt(squares / width_all + NORM_EPSILON) * gain_ref[...]
    normed = jnp.concatenate([normed, jnp.zeros((PADR - rows, width), F32)], axis=0)
    outgoing = dot(chooser, normed.astype(BF16)).astype(BF16)
    for e in range(ngrp):
        outg[e] = outgoing[e * SLOT : (e + 1) * SLOT]

    copies = [
        push(outg.at[lax.rem(z + d, nz) // nzl], zin.at[d], at_z(d)) for d in range(1, nz)
    ]
    zin[0] = outg[g]
    for copy in copies:
        copy.wait_recv()
    packed = iota((hr, nz * SLOT), 0)
    padded = iota((hr, nz * SLOT), 1)
    match = (packed // CAP == padded // SLOT) & (packed % CAP == padded % SLOT)
    pack = match.astype(F32).astype(BF16)
    xin[0, 0] = dot(pack, zin[...].reshape(nz * SLOT, width)).astype(BF16)

    core_copy = {0: push(xin.at[0, 0], xin.at[0, 1], sibling)}
    x_copy = {
        1: push(xin.at[0, 0], xin.at[1, 0], at_x(1)),
        3: push(xin.at[0, 0], xin.at[3, 0], at_x(3)),
    }
    relay = []
    low, high = pl.ds(0, hh), pl.ds(hh, hh)

    def task_x1():
        x_copy[1].wait_recv()
        relay.append(push(xin.at[1, 0, low], xin.at[2, 0, low], at_x(1)))
        core_copy[1] = push(xin.at[1, 0], xin.at[1, 1], sibling)
        x_copy[3].wait_recv()
        relay.append(push(xin.at[3, 0, high], xin.at[2, 0, high], at_x(3)))
        core_copy[3] = push(xin.at[3, 0], xin.at[3, 1], sibling)

    def task_x2():
        for copy in relay:
            copy.wait_recv()
        core_copy[2] = push(xin.at[2, 0], xin.at[2, 1], sibling)

    def block(o):
        return lax.rem(t + o + nt, nt)

    rs = {}

    def task_m1(c):
        if c == 0:
            loads[2].wait()
            loads[3].wait()
        core_copy[c].wait_recv()
        slots = xin[c].reshape(2 * hr, width)
        for part, weight in enumerate((wg, wu)):
            result = dot(slots, weight[...]).astype(BF16)
            for b in range(nb):
                for h in range(2):
                    pre[c, 2 * b + h, part] = result[
                        h * hr : (h + 1) * hr, b * HD : (b + 1) * HD
                    ]
        far = block(half)
        rs[c] = (
            push(pre.at[c, far, 0], rs_in.at[c, 0, 0, 0], at_t(1)),
            push(pre.at[c, far, 1], rs_in.at[c, 1, 0, 1], at_t(nt - 1)),
        )

    def task_rs(c, step):
        down = block(half - step)
        up = block(step - half)
        out = []
        for way, (copy, here, to) in enumerate(
            zip(rs[c], (down, up), (at_t(1), at_t(nt - 1)))
        ):
            copy.wait_recv()
            if step == 1:
                pre[c, here, way] = (
                    pre[c, here, way].astype(F32) + rs_in[c, way, 0, way].astype(F32)
                ).astype(BF16)
            else:
                pre[c, here] = (
                    pre[c, here].astype(F32) + rs_in[c, way, step - 1].astype(F32)
                ).astype(BF16)
            out.append(push(pre.at[c, here], rs_in.at[c, way, step], to))
        rs[c] = tuple(out)

    ag = {}

    def task_silu(c):
        for copy in rs[c]:
            copy.wait_recv()
        total = pre[c, t].astype(F32)
        if half > 1:
            total = total + rs_in[c, 0, half - 1].astype(F32)
            total = total + rs_in[c, 1, half - 1].astype(F32)
            gate, up = total[0], total[1]
        else:
            gate = total[0] + rs_in[c, 0, 0, 0].astype(F32)
            up = total[1] + rs_in[c, 1, 0, 1].astype(F32)
        act[c, t] = (gate / (1.0 + jnp.exp(-gate)) * up).astype(BF16)
        send_act(c, 0)

    def send_act(c, hop):
        right = act.at[c, block(-hop)]
        left = act.at[c, block(hop)]
        if hop == half - 1:
            right, left = right.at[low], left.at[high]
        ag[c] = (push(right, right, at_t(1)), push(left, left, at_t(nt - 1)))

    def task_ag(c, hop):
        for copy in ag[c]:
            copy.wait_recv()
        send_act(c, hop)

    def task_m2(c):
        if c == 0:
            loads[4].wait()
        for copy in ag[c]:
            copy.wait_recv()
        for h in (1, 0):
            units = jnp.concatenate([act[c, 2 * b + h] for b in range(nb)], axis=1)
            outp[c, h] = dot(units, wd[...]).astype(BF16)
            if h == 1:
                core_copy[c] = push(outp.at[c, 1], core_in.at[c], sibling)

    def task_core(c):
        core_copy[c].wait_recv()
        ysum[c] = (outp[c, 0].astype(F32) + core_in[c].astype(F32)).astype(BF16)
        if c == 2:
            halves.append(push(ysum.at[2, low], half_in.at[0], at_x(3)))
            halves.append(push(ysum.at[2, high], half_in.at[1], at_x(1)))

    halves = []
    x_back = []

    def task_x_back():
        for way, (c, part, to) in enumerate(((1, low, at_x(3)), (3, high, at_x(1)))):
            halves[way].wait_recv()
            ysum[c, part] = (ysum[c, part].astype(F32) + half_in[way].astype(F32)).astype(BF16)
            x_back.append(push(ysum.at[c], full_in.at[way], to))

    stages = [task_m1]
    stages += [functools.partial(task_rs, step=s) for s in range(1, half)]
    stages += [task_silu]
    stages += [functools.partial(task_ag, hop=h) for h in range(1, half)]
    stages += [task_m2, task_core]
    for k in range(len(stages) + 2 * (NX - 1)):
        for c in range(NX):
            if 0 <= k - 2 * c < len(stages):
                stages[k - 2 * c](c)
        if k == 1:
            task_x1()
        if k == 3:
            task_x2()
    task_x_back()
    for copy in x_back:
        copy.wait_recv()
    mine = (
        ysum[0].astype(F32) + full_in[0].astype(F32) + full_in[1].astype(F32)
    ).astype(BF16)
    spread = lax.dot_general(pack, mine, (((0,), (0,)), ((), ())), preferred_element_type=F32)
    zsend[...] = spread.astype(BF16).reshape(nz, SLOT, width)

    copies = [push(zsend.at[d], zback.at[d], at_z(nz - d)) for d in range(1, nz)]
    zback[0] = zsend[0]
    for copy in copies:
        copy.wait_recv()
    experts = [jnp.zeros((SLOT, width), F32) for e in range(ngrp)]
    for d in range(nz):
        expert = lax.rem(z + d, nz) // nzl
        piece = zback[d].astype(F32)
        for e in range(ngrp):
            experts[e] = experts[e] + piece * (expert == e).astype(F32)
    brought = jnp.concatenate(experts, axis=0).astype(BF16)
    gate_high = gating.astype(BF16)
    gate_low = (gating - gate_high.astype(F32)).astype(BF16)
    expert_sum = dot(gate_high, brought) + dot(gate_low, brought)
    out_ref[...] = (hid[...] + expert_sum[0:rows]).astype(BF16)

    for copy in sent:
        copy.wait_send()


def local(
    sizes,
    queries,
    new_keys,
    new_values,
    key_pages,
    value_pages,
    page_order,
    page_counts,
    residual,
    norm_gain,
    routes,
    route_weights,
    w_gate,
    w_up,
    w_down,
):
    nattn, ngrp, nt, width_all = sizes
    rows, width = queries.shape
    heads = width // HD
    pool = key_pages.shape[0]
    units = w_gate.shape[2]
    nzl = nattn // (NX * NCORE)
    nz = nzl * ngrp
    hr = nz * CAP
    half = nt // 2
    pieces = pool // 16
    copies = 200
    vmem = pl.BlockSpec(memory_space=pltpu.VMEM)
    hbm = pl.BlockSpec(memory_space=pl.ANY)
    return pl.pallas_call(
        functools.partial(kernel, sizes),
        out_shape=jax.ShapeDtypeStruct((rows, width), BF16),
        in_specs=[vmem] * 9 + [hbm] * 5,
        out_specs=vmem,
        scratch_shapes=[
            pltpu.VMEM((pool, PAGE, 2 * HD), BF16),
            pltpu.VMEM((pool, PAGE, HD), BF16),
            pltpu.VMEM((width, units), BF16),
            pltpu.VMEM((width, units), BF16),
            pltpu.VMEM((units, width), BF16),
            pltpu.VMEM((pieces, heads * rows, 16 * PAGE), F32),
            pltpu.VMEM((8, HD), F32),
            pltpu.VMEM((nt, 8, HD), F32),
            pltpu.VMEM((rows, width), F32),
            pltpu.VMEM((ngrp, SLOT, width), BF16),
            pltpu.VMEM((nz, SLOT, width), BF16),
            pltpu.VMEM((NX, 2, hr, width), BF16),
            pltpu.VMEM((NX, nt, 2, hr, HD), BF16),
            pltpu.VMEM((NX, 2, half, 2, hr, HD), BF16),
            pltpu.VMEM((NX, nt, hr, HD), BF16),
            pltpu.VMEM((NX, 2, hr, width), BF16),
            pltpu.VMEM((NX, hr, width), BF16),
            pltpu.VMEM((NX, hr, width), BF16),
            pltpu.VMEM((2, hr // 2, width), BF16),
            pltpu.VMEM((2, hr, width), BF16),
            pltpu.VMEM((nz, SLOT, width), BF16),
            pltpu.VMEM((nz, SLOT, width), BF16),
            pltpu.SemaphoreType.DMA((5,)),
            pltpu.SemaphoreType.DMA((copies,)),
            pltpu.SemaphoreType.DMA((copies,)),
        ],
        compiler_params=pltpu.CompilerParams(
            collective_id=0, has_side_effects=True, vmem_limit_bytes=48 * 1024 * 1024
        ),
    )(
        queries,
        new_keys,
        new_values,
        page_order,
        page_counts,
        residual,
        norm_gain.reshape(1, width),
        routes.T,
        route_weights.T,
        key_pages,
        value_pages,
        w_gate,
        w_up,
        w_down,
    )


def solution(mesh):
    sizes = (mesh.shape["attn"], mesh.shape["grp"], mesh.shape["tp"])

    def whole(*arrays):
        return jax.shard_map(
            functools.partial(local, sizes + (arrays[0].shape[1],)),
            mesh=mesh,
            in_specs=(
                P(("attn", "grp"), "tp"),
                P(("attn", "grp"), "tp"),
                P(("attn", "grp"), "tp"),
                P(("attn", "grp"), None, "tp"),
                P(("attn", "grp"), None, "tp"),
                P(("attn", "grp"), None),
                P(("attn", "grp"), None),
                P(("attn", "grp"), "tp"),
                P("tp"),
                P(("attn", "grp"), None),
                P(("attn", "grp"), None),
                P("grp", "tp", "attn"),
                P("grp", "tp", "attn"),
                P("grp", "attn", "tp"),
            ),
            out_specs=P(("attn", "grp"), "tp"),
            check_vma=False,
        )(*arrays)

    return whole
```

time: 386 us -> 106 us (0.27)
  waiting for transfers between devices: 297 us -> 0 us
  Pallas kernels: 0 us -> 95.9 us
  blocking collectives: 31.8 us -> 0 us
  between operations: 13.3 us -> 0.07 us
  matrix products: 11.7 us -> 0 us
  local copies, waits for them, and re-layouts: 17.6 us -> 9.4 us
  starting transfers between devices: 6.05 us -> 0 us
  other arithmetic: 3.9 us -> 0 us
    reduce_scatter x1 -> x0, waiting for transfers between devices: 147 us -> none  [local(): lax.psum_scatter(jnp.dot(active, down_block, preferred_element_type=jnp.f...]
    pallas_call x0 -> x1, Pallas kernels: none -> 95.9 us  [local(): pl.pallas_call(functools.partial(kernel, sizes), out_shape=jax.ShapeDtype...]
    psum x1 -> x0, waiting for transfers between devices: 78.7 us -> none  [local(): lax.psum(jnp.dot(slots_in, joined, preferred_element_type=jnp.float32).as...]
    all_gather x1 -> x0, waiting for transfers between devices: 64.3 us -> none  [local(): slots_in = lax.all_gather(arrived, 'attn', axis=0, tiled=True)]
    all_to_all x1 -> x0, blocking collectives: 16.9 us -> none  [local(): lax.all_to_all(outgoing, 'grp', split_axis=0, concat_axis=0, tiled=True)]
    psum x1 -> x0, blocking collectives: 14.8 us -> none  [local(): squares = lax.psum(jnp.sum(hidden_wide * hidden_wide, axis=1), 'tp')]
    gather x4 -> x0, local copies, waits for them, and re-layouts: 12.1 us -> none  [the longest x2 5.05 us: attend(): pages = order[offsets]]
    dot_general x7 -> x0, matrix products: 11.7 us -> none  [the longest x1 3.66 us: local(): jnp.dot(slots_in, joined, preferred_element_type=jnp.float32)]
  transfers between devices with their start and end apart: 4 -> 0, of which waited for: 4 -> 0; matrix products, arithmetic and copies ran while one was open for 0% -> 0% of each run, Pallas kernels for 0% -> 0%
where the time goes in v1:
time: 106 us; the launch traced here: 105 us
  Pallas kernels  95.9 us (90%)
  local copies, waits for them, and re-layouts  9.4 us (9%)
    pallas_call x1, Pallas kernels, local(): pl.pallas_call(functools.partial(kernel, sizes), out_shape=jax.ShapeDtype...  95.9 us
    unnamed x27, local copies, waits for them, and re-layouts  8.66 us

profile of v1, /device:TPU:1, one launch (start us, length us, event | category | flops | bytes accessed | tf_op | source)
XLA Modules:
  0.0 105.3 jit_solution(8161072600236658607)
XLA Ops:
  0.0 0.0 copy-start.7
  0.0 0.0 copy-start.9
  0.0 0.0 copy-start.10
  0.0 0.0 copy-start.11
  0.0 0.0 copy-start.12
  0.0 0.7 reshape.3.gain_ref
  0.8 0.0 copy-done.7
  0.8 0.0 copy-done.9
  0.8 0.0 copy-done.10
  0.8 0.0 copy-done.11
  0.8 0.0 copy-done.12
  0.8 0.0 copy-start
  0.8 1.2 %copy-done = bf16[240,16,128]{2,1,0:T(8,128)(2,1)S(1)} copy-done((bf16[240,16,128]{2,1,0:T(8,128)(2,1)S(1)}, bf16[240,16,128]{2,1,0:T(8,128)(2,1)}, u32[]{:S(2)}) %copy-start) | copy-done | bytes 983064
  2.0 0.0 copy-start.1
  2.0 1.2 %copy-done.1 = bf16[240,16,128]{2,1,0:T(8,128)(2,1)S(1)} copy-done((bf16[240,16,128]{2,1,0:T(8,128)(2,1)S(1)}, bf16[240,16,128]{2,1,0:T(8,128)(2,1)}, u32[]{:S(2)}) %copy-start.1) | copy-done | bytes 983064
  3.2 0.0 copy-start.2
  3.2 1.1 %copy-done.2 = bf16[1,768,512]{2,1,0:T(8,128)(2,1)S(1)} copy-done((bf16[1,768,512]{2,1,0:T(8,128)(2,1)S(1)}, bf16[1,768,512]{2,1,0:T(8,128)(2,1)}, u32[]{:S(2)}) %copy-start.2) | copy-done | bytes 786456
  4.3 0.0 copy-start.3
  4.3 1.1 %copy-done.3 = bf16[1,768,512]{2,1,0:T(8,128)(2,1)S(1)} copy-done((bf16[1,768,512]{2,1,0:T(8,128)(2,1)S(1)}, bf16[1,768,512]{2,1,0:T(8,128)(2,1)}, u32[]{:S(2)}) %copy-start.3) | copy-done | bytes 786456
  5.5 0.0 copy-start.4
  5.5 1.1 %copy-done.4 = bf16[1,512,768]{2,1,0:T(8,128)(2,1)S(1)} copy-done((bf16[1,512,768]{2,1,0:T(8,128)(2,1)S(1)}, bf16[1,512,768]{2,1,0:T(8,128)(2,1)}, u32[]{:S(2)}) %copy-start.4) | copy-done | bytes 786456
  6.6 0.0 copy-start.5
  6.6 0.8 copy-done.5
  7.4 0.0 copy-start.6
  7.4 0.8 copy-done.6
  8.1 0.0 copy-start.8
  8.1 0.7 copy-done.8
  8.8 95.9 %shard_map.136 = bf16[24,768]{1,0:T(8,128)(2,1)S(1)} custom-call(bf16[24,768]{1,0:T(8,128)(2,1)S(1)} %copy-done.5, bf16[24,128]{1,0:T(8,128)(2,1)S(1)} %copy-done.7, bf16[24,128]{1,0:T(8,128)(2,1)S(1)} %copy-done.8, s32[1,240]{1,0:T(1,128)S(1)} %copy-done.9, s32[1,24]{1,0:T(1,128)S(1)} %copy-done.12, bf16[24,768]{1,0:T(8,128)(2,1)S(1)} %copy-done.6, ...), custom_call_target="tpu_custom_call" | custom-call | tf_op jit(solution)/shard_map/pallas_call | solution.py:467
  104.7 0.6 copy.16
Async XLA Ops:
  0.0 0.8 copy-start.7
  0.0 0.8 copy-start.9
  0.0 0.8 copy-start.10
  0.0 0.8 copy-start.11
  0.0 0.8 copy-start.12
  0.8 1.2 %copy-start = (bf16[240,16,128]{2,1,0:T(8,128)(2,1)S(1)}, bf16[240,16,128]{2,1,0:T(8,128)(2,1)}, u32[]{:S(2)}) copy-start(bf16[240,16,128]{2,1,0:T(8,128)(2,1)} %k_hbm.1) | copy-start | bytes 2949124
  2.0 1.2 %copy-start.1 = (bf16[240,16,128]{2,1,0:T(8,128)(2,1)S(1)}, bf16[240,16,128]{2,1,0:T(8,128)(2,1)}, u32[]{:S(2)}) copy-start(bf16[240,16,128]{2,1,0:T(8,128)(2,1)} %v_hbm.1) | copy-start | bytes 2949124
  3.2 1.1 %copy-start.2 = (bf16[1,768,512]{2,1,0:T(8,128)(2,1)S(1)}, bf16[1,768,512]{2,1,0:T(8,128)(2,1)}, u32[]{:S(2)}) copy-start(bf16[1,768,512]{2,1,0:T(8,128)(2,1)} %wg_hbm.1) | copy-start | bytes 2359300
  4.3 1.1 %copy-start.3 = (bf16[1,768,512]{2,1,0:T(8,128)(2,1)S(1)}, bf16[1,768,512]{2,1,0:T(8,128)(2,1)}, u32[]{:S(2)}) copy-start(bf16[1,768,512]{2,1,0:T(8,128)(2,1)} %wu_hbm.1) | copy-start | bytes 2359300
  5.5 1.1 %copy-start.4 = (bf16[1,512,768]{2,1,0:T(8,128)(2,1)S(1)}, bf16[1,512,768]{2,1,0:T(8,128)(2,1)}, u32[]{:S(2)}) copy-start(bf16[1,512,768]{2,1,0:T(8,128)(2,1)} %wd_hbm.1) | copy-start | bytes 2359300
  6.6 0.8 copy-start.5
  7.4 0.8 copy-start.6
  8.1 0.7 copy-start.8

commit v2 on v1

v2 whole, which is shorter than its diff:
```python
import functools
import math

import jax
import jax.numpy as jnp
from jax import lax
from jax.experimental import pallas as pl
from jax.experimental.pallas import tpu as pltpu
from jax.sharding import PartitionSpec as P

HD = 128
PAGE = 16
CAP = 12
SLOT = 16
PADR = 32
NX = 4
NCORE = 2
NORM_EPSILON = 1e-05
MASKED = -1e30
MESH = pl.DeviceIdType.MESH
IN, M1, RS2, SILU, AG2, M2, HOME, BACK = range(8)
ORDER = (
    (IN, 0), (M1, 0), (IN, 7), (M1, 7), (IN, 2), (IN, 3), (RS2, 0), (IN, 1), (M1, 2), (IN, 5),
    (M1, 1), (M1, 3), (IN, 4), (M1, 5), (IN, 6), (M1, 6), (M1, 4), (RS2, 3), (RS2, 5),
    (RS2, 2), (RS2, 6), (RS2, 1), (SILU, 3), (RS2, 4), (SILU, 5), (SILU, 2), (SILU, 6),
    (RS2, 7), (AG2, 3), (SILU, 1), (SILU, 4), (SILU, 0), (AG2, 6), (AG2, 5), (AG2, 2),
    (SILU, 7), (M2, 3), (AG2, 1), (AG2, 4), (HOME, 3), (AG2, 0), (M2, 6), (M2, 5), (M2, 2),
    (HOME, 6), (AG2, 7), (HOME, 2), (M2, 1), (HOME, 5), (M2, 4), (HOME, 1), (M2, 0), (HOME, 4),
    (M2, 7), (BACK, 0), (BACK, 1),
)
F32 = jnp.float32
BF16 = jnp.bfloat16


def z_groups(nz):
    if nz == 2:
        return ((0,), (1,))
    quarter = nz // 4
    near = tuple(range(quarter + 1)) + tuple(range(nz - quarter + 1, nz))
    return near, tuple(d for d in range(nz) if d not in near)


def iota(shape, dim):
    return lax.broadcasted_iota(jnp.int32, shape, dim)


def to_column(row, rows, start=0):
    n = row.shape[1]
    eye = iota((rows, n), 0) + start == iota((rows, n), 1)
    return jnp.sum(jnp.where(eye, row, jnp.zeros_like(row)), axis=1, keepdims=True)


def to_row(column, lanes, start=0):
    n = column.shape[0]
    eye = iota((n, lanes), 0) + start == iota((n, lanes), 1)
    return jnp.sum(jnp.where(eye, column, jnp.zeros_like(column)), axis=0, keepdims=True)


def before(column, lanes):
    n = column.shape[0]
    ahead = iota((n, lanes), 0) < iota((n, lanes), 1)
    return jnp.sum(jnp.where(ahead, column, jnp.zeros_like(column)), axis=0, keepdims=True)


def dot(a, b):
    return jnp.dot(a, b, preferred_element_type=F32)


def kernel(
    sizes,
    q_hbm,
    nk_hbm,
    nv_hbm,
    order_hbm,
    counts_hbm,
    res_hbm,
    gain_hbm,
    routes_hbm,
    rw_hbm,
    k_hbm,
    v_hbm,
    wg_hbm,
    wu_hbm,
    wd_hbm,
    out_ref,
    q_ref,
    nk_ref,
    nv_ref,
    order_ref,
    counts_ref,
    res_ref,
    gain_ref,
    routes_ref,
    rw_ref,
    kaug,
    vbuf,
    wg,
    wu,
    wd,
    scores,
    sq_own,
    sq_in,
    hid,
    outg,
    zin,
    xin,
    pre,
    rs_half,
    rs_in,
    act,
    outp,
    core_in,
    xsend,
    xback,
    zsend,
    zback,
    local_sems,
    send_sems,
    recv_sems,
):
    nattn, ngrp, nt, width_all = sizes
    rows, width = q_ref.shape
    heads = width // HD
    pool = order_ref.shape[1]
    nzl = nattn // (NX * NCORE)
    nz = nzl * ngrp
    groups = z_groups(nz)
    steps = [0, 1] + list(range(NX - 1, 1, -1))
    chunks = [(dx, 0) for dx in steps] + [(dx, 1) for dx in steps[1:] + [0]]
    index = {chunk: c for c, chunk in enumerate(chunks)}
    nd = nz // 2
    hr = nd * CAP
    nb = nt // 2

    a = lax.axis_index("attn")
    g = lax.axis_index("grp")
    t = lax.axis_index("tp")
    core = lax.rem(a, NCORE)
    zl = lax.rem(a // NCORE, nzl)
    x = a // (NCORE * nzl)
    z = g * nzl + zl

    def at_xz(c, d):
        to = lax.rem(z + d, nz)
        return {
            "attn": (lax.rem(x + c, NX) * nzl + lax.rem(to, nzl)) * NCORE + core,
            "grp": to // nzl,
            "tp": t,
        }

    def at_t(d):
        return {"attn": a, "grp": g, "tp": lax.rem(t + d + nt, nt)}

    sibling = {"attn": a + 1 - 2 * core, "grp": g, "tp": t}

    pairs = [
        (counts_hbm, counts_ref),
        (order_hbm, order_ref),
        (q_hbm, q_ref),
        (nk_hbm, nk_ref),
        (k_hbm, kaug.at[:, :, pl.ds(0, HD)]),
        (v_hbm, vbuf),
        (nv_hbm, nv_ref),
        (res_hbm, res_ref),
        (routes_hbm, routes_ref),
        (rw_hbm, rw_ref),
        (gain_hbm, gain_ref.at[0]),
        (wg_hbm.at[0], wg),
        (wu_hbm.at[0], wu),
        (wd_hbm.at[0], wd),
    ]
    loads = []
    for i, (src, dst) in enumerate(pairs):
        loads.append(pltpu.make_async_copy(src, dst, local_sems.at[i]))
        loads[i].start()

    barrier = pltpu.get_barrier_semaphore()
    partners = [at_t(d) for d in range(1, nt)] + [sibling]
    partners += [at_xz(dx, 0) for dx in range(1, NX)] + [at_xz(0, d) for d in range(1, nz)]
    for partner in partners:
        pl.semaphore_signal(barrier, inc=1, device_id=partner, device_id_type=MESH)

    for i in range(4):
        loads[i].wait()

    sent = []

    def push(src, dst, to):
        index = len(sent)
        copy = pltpu.make_async_remote_copy(
            src_ref=src,
            dst_ref=dst,
            send_sem=send_sems.at[index],
            recv_sem=recv_sems.at[index],
            device_id=to,
            device_id_type=MESH,
        )
        copy.start()
        sent.append(copy)
        return copy

    counts_col = to_column(counts_ref[...].astype(F32), rows)
    starts_row = before(counts_col, HD)
    counts_row = to_row(counts_col, HD)
    place = iota((pool, HD), 0).astype(F32)
    row_of_place = ((place >= starts_row) & (place < starts_row + counts_row)).astype(F32)
    place_of_page = (iota((pool, pool), 0) == order_ref[...]).astype(F32)
    owner = dot(place_of_page.astype(BF16), row_of_place.astype(BF16))
    kaug[:, :, pl.ds(HD, HD)] = jnp.broadcast_to(
        owner.reshape(pool, 1, HD), (pool, PAGE, HD)
    ).astype(BF16)
    own_row = iota((rows, HD), 0)
    lane = iota((rows, HD), 1)
    mask_block = jnp.where((own_row == lane) | (lane >= rows), 0.0, MASKED)

    q_wide = q_ref[...].astype(F32)
    q_rows = jnp.concatenate([q_wide[:, h * HD : (h + 1) * HD] for h in range(heads)], axis=0)
    q_aug = jnp.concatenate(
        [q_rows, jnp.concatenate([mask_block] * heads, axis=0)], axis=1
    ).astype(BF16)
    scale = 1.0 / math.sqrt(HD)
    new_key = jnp.concatenate([nk_ref[...].astype(F32)] * heads, axis=0)
    own = jnp.sum(q_rows * new_key, axis=1, keepdims=True) * scale

    loads[4].wait()
    pieces = scores.shape[0]
    pages = pool // pieces
    tokens = pages * PAGE

    def score_piece(i, top):
        keys = kaug[pl.ds(i * pages, pages)].reshape(tokens, 2 * HD)
        piece = (
            lax.dot_general(
                q_aug, keys, (((1,), (1,)), ((), ())), preferred_element_type=F32
            )
            * scale
        )
        scores[i] = piece
        return jnp.maximum(top, piece)

    top = lax.fori_loop(
        0, pieces, score_piece, jnp.full((heads * rows, tokens), MASKED, F32), unroll=True
    )
    top = jnp.maximum(jnp.max(top, axis=1, keepdims=True), own)
    own_weight = jnp.exp(own - top)

    loads[5].wait()

    def value_piece(i, carry):
        total, mixed = carry
        weights = jnp.exp(scores[i] - top)
        values = vbuf[pl.ds(i * pages, pages)].reshape(tokens, HD)
        return total + weights, mixed + dot(weights.astype(BF16), values)

    total, mixed = lax.fori_loop(
        0,
        pieces,
        value_piece,
        (jnp.zeros((heads * rows, tokens), F32), jnp.zeros((heads * rows, HD), F32)),
        unroll=True,
    )
    total = jnp.sum(total, axis=1, keepdims=True) + own_weight
    for i in range(6, 11):
        loads[i].wait()
    own_low = own_weight.astype(BF16).astype(F32)
    new_value = jnp.concatenate([nv_ref[...].astype(F32)] * heads, axis=0)
    attention = (mixed + own_low * new_value) / total
    attention = jnp.concatenate(
        [attention[h * rows : (h + 1) * rows] for h in range(heads)], axis=1
    )
    hidden = (res_ref[...].astype(F32) + attention).astype(BF16).astype(F32)
    hid[...] = hidden
    routes = routes_ref[...]
    route_weights = rw_ref[...]
    chosen, gated = [], []
    for e in range(ngrp):
        named = routes == e
        hit_row = jnp.max(named.astype(F32), axis=0, keepdims=True)
        gate_row = jnp.sum(jnp.where(named, route_weights, 0.0), axis=0, keepdims=True)
        hit_col = to_column(hit_row, PADR)
        gate_col = to_column(gate_row, PADR)
        pos_row = before(hit_col, PADR)
        pos_col = to_column(pos_row, PADR)
        hit_wide = to_row(hit_col, PADR)
        slot = iota((SLOT, PADR), 0).astype(F32)
        chosen.append(jnp.where(slot == pos_row, hit_wide, 0.0))
        slot = iota((PADR, SLOT), 1).astype(F32)
        gated.append(jnp.where(slot == pos_col, hit_col * gate_col, 0.0))
    chooser = jnp.concatenate(chosen, axis=0).astype(BF16)
    gating = jnp.concatenate(gated, axis=1)

    pl.semaphore_wait(barrier, len(partners))

    padding = jnp.zeros((PADR - rows, width), F32)
    padded_rows = jnp.concatenate([hid[...], padding], axis=0).astype(BF16)
    outgoing = dot(chooser, padded_rows).astype(BF16)
    for e in range(ngrp):
        outg[e] = outgoing[e * SLOT : (e + 1) * SLOT]

    zin_copy, x_copy = {}, {}
    for group in range(2):
        for i, d in enumerate(groups[group]):
            if d:
                expert = lax.rem(z + d, nz) // nzl
                zin_copy[group, i] = push(outg.at[expert], zin.at[group, i], at_xz(0, d))
    zin[0, 0] = outg[g]
    packed = iota((hr, nd * SLOT), 0)
    padded = iota((hr, nd * SLOT), 1)
    match = (packed // CAP == padded // SLOT) & (packed % CAP == padded % SLOT)
    pack = match.astype(F32).astype(BF16)
    gain = gain_ref[...]

    core_copy, rs, sq_copy, ag, home = {}, {}, {}, {}, {}
    seen, squared = set(), set()

    def block(o):
        return lax.rem(t + o + nt, nt)

    def task_in(c):
        dx, group = chunks[c]
        if dx == 0:
            for i, d in enumerate(groups[group]):
                if d:
                    zin_copy[group, i].wait_recv()
            xin[c, 0] = dot(pack, zin[group].reshape(nd * SLOT, width)).astype(BF16)
            core_copy[c] = push(xin.at[c, 0], xin.at[c, 1], sibling)
            for to in steps[1:]:
                far = index[to, group]
                x_copy[far] = push(xin.at[c, 0], xin.at[far, 0], at_xz(to, 0))
        else:
            x_copy[c].wait_recv()
            core_copy[c] = push(xin.at[c, 0], xin.at[c, 1], sibling)

    def task_m1(c):
        core_copy[c].wait_recv()
        slots = xin[c].reshape(2 * hr, width).astype(F32)
        gained = (slots * gain).astype(BF16)
        for part, weight in enumerate((wg, wu)):
            result = dot(gained, weight[...]).astype(BF16)
            for b in range(nb):
                for h in range(2):
                    pre[c, 2 * b + h, part] = result[
                        h * hr : (h + 1) * hr, b * HD : (b + 1) * HD
                    ]
        far = block(4)
        rs[c] = [
            push(pre.at[c, far, 0], rs_half.at[c, 0], at_t(2)),
            push(pre.at[c, far, 1], rs_half.at[c, 1], at_t(-2)),
            push(pre.at[c, block(3)], rs_in.at[c, 0], at_t(1)),
            push(pre.at[c, block(-3)], rs_in.at[c, 1], at_t(-1)),
            push(pre.at[c, block(1)], rs_in.at[c, 2], at_t(1)),
            push(pre.at[c, block(-1)], rs_in.at[c, 3], at_t(-1)),
        ]
        dx, group = chunks[c]
        squares = jnp.sum(slots * slots, axis=1, keepdims=True)
        for h in range(2):
            row = to_row(squares[h * hr : (h + 1) * hr], HD, group * hr)
            sq_own[dx, h] = sq_own[dx, h] + row if dx in seen else row
        if dx in seen:
            sq_copy[dx] = [
                push(sq_own.at[dx, lax.rem(t + d, 2)], sq_in.at[dx, d], at_t(d))
                for d in range(1, nt)
            ]
        seen.add(dx)

    def task_rs2(c):
        out = []
        for way, (here, to) in enumerate(((block(2), at_t(2)), (block(-2), at_t(-2)))):
            rs[c][way].wait_recv()
            rs[c][2 + way].wait_recv()
            near = rs_in[c, way].astype(F32)
            pre[c, here, way] = (
                pre[c, here, way].astype(F32) + near[way] + rs_half[c, way].astype(F32)
            ).astype(BF16)
            other = 1 - way
            pre[c, here, other] = (pre[c, here, other].astype(F32) + near[other]).astype(BF16)
            out.append(push(pre.at[c, here], rs_in.at[c, 4 + way], to))
        rs[c] = rs[c][4:] + out

    def task_silu(c):
        dx, group = chunks[c]
        for copy in rs[c] + ([] if dx in squared else sq_copy[dx]):
            copy.wait_recv()
        squared.add(dx)
        squares = sq_own[dx, lax.rem(t, 2)]
        for d in range(1, nt):
            squares = squares + sq_in[dx, d]
        scale_row = lax.rsqrt(squares / width_all + NORM_EPSILON)
        scale = to_column(scale_row, hr, group * hr)
        total = pre[c, t].astype(F32)
        for i in range(2, 6):
            total = total + rs_in[c, i].astype(F32)
        gate, up = total[0] * scale, total[1] * scale
        act[c, t] = (gate / (1.0 + jnp.exp(-gate)) * up).astype(BF16)
        own = act.at[c, t]
        ag[c] = [push(own, own, at_t(d)) for d in (2, -2, 1, -1)]

    def task_ag2(c):
        out = []
        for way, d in enumerate((2, -2)):
            ag[c][way].wait_recv()
            arrived = act.at[c, block(-d)]
            if way == c % 2:
                out.append(push(arrived, arrived, at_t(d)))
            out.append(push(arrived, arrived, at_t(d // 2)))
        ag[c] = ag[c][2:] + out

    def task_m2(c):
        for copy in ag[c]:
            copy.wait_recv()
        for h in (1, 0):
            units = jnp.concatenate([act[c, 2 * b + h] for b in range(nb)], axis=1)
            outp[c, h] = dot(units, wd[...]).astype(BF16)
            if h == 1:
                core_copy[c] = push(outp.at[c, 1], core_in.at[c], sibling)

    def both_cores(c):
        core_copy[c].wait_recv()
        return outp[c, 0].astype(F32) + core_in[c].astype(F32)

    def task_home(c):
        dx, group = chunks[c]
        xsend[c] = both_cores(c).astype(BF16)
        x_copy[c] = push(xsend.at[c], xback.at[c], at_xz(NX - dx, 0))

    def task_back(group):
        total = both_cores(index[0, group])
        for dx in steps[1:]:
            c = index[dx, group]
            x_copy[c].wait_recv()
            total = total + xback[c].astype(F32)
        spread = lax.dot_general(
            pack, total.astype(BF16), (((0,), (0,)), ((), ())), preferred_element_type=F32
        )
        zsend[group] = spread.astype(BF16).reshape(nd, SLOT, width)
        for i, d in enumerate(groups[group]):
            if d:
                home[group, i] = push(
                    zsend.at[group, i], zback.at[group, i], at_xz(0, nz - d)
                )
            else:
                zback[group, i] = zsend[group, i]

    tasks = (task_in, task_m1, task_rs2, task_silu, task_ag2, task_m2, task_home, task_back)
    for i in range(11, 14):
        loads[i].wait()
    for task, c in ORDER:
        if c < len(chunks) and (task != HOME or chunks[c][0]):
            tasks[task](c)
    for copy in sent[:-nz]:
        copy.wait_send()

    sums = [None] * nz
    for group in range(2):
        for i, d in enumerate(groups[group]):
            if d:
                home[group, i].wait_recv()
            sums[d] = zback[group, i].astype(F32)
    experts = [jnp.zeros((SLOT, width), F32) for e in range(ngrp)]
    for d in range(nz):
        expert = lax.rem(z + d, nz) // nzl
        for e in range(ngrp):
            experts[e] = experts[e] + sums[d] * (expert == e).astype(F32)
    brought = jnp.concatenate(experts, axis=0).astype(BF16)
    gate_high = gating.astype(BF16)
    gate_low = (gating - gate_high.astype(F32)).astype(BF16)
    expert_sum = dot(gate_high, brought) + dot(gate_low, brought)
    out_ref[...] = (hid[...] + expert_sum[0:rows]).astype(BF16)

    for copy in sent[-nz:]:
        copy.wait_send()


def local(
    sizes,
    queries,
    new_keys,
    new_values,
    key_pages,
    value_pages,
    page_order,
    page_counts,
    residual,
    norm_gain,
    routes,
    route_weights,
    w_gate,
    w_up,
    w_down,
):
    nattn, ngrp, nt, width_all = sizes
    rows, width = queries.shape
    heads = width // HD
    pool = key_pages.shape[0]
    units = w_gate.shape[2]
    nzl = nattn // (NX * NCORE)
    nz = nzl * ngrp
    nc, nd = NX * 2, nz // 2
    hr = nd * CAP
    pieces = pool // 16
    copies = 320
    vmem = pl.BlockSpec(memory_space=pltpu.VMEM)
    hbm = pl.BlockSpec(memory_space=pltpu.HBM)
    return pl.pallas_call(
        functools.partial(kernel, sizes),
        out_shape=jax.ShapeDtypeStruct((rows, width), BF16),
        in_specs=[hbm] * 14,
        out_specs=vmem,
        scratch_shapes=[
            pltpu.VMEM((rows, width), BF16),
            pltpu.VMEM((rows, HD), BF16),
            pltpu.VMEM((rows, HD), BF16),
            pltpu.VMEM((1, pool), jnp.int32),
            pltpu.VMEM((1, rows), jnp.int32),
            pltpu.VMEM((rows, width), BF16),
            pltpu.VMEM((1, width), F32),
            pltpu.VMEM((2, rows), jnp.int32),
            pltpu.VMEM((2, rows), F32),
            pltpu.VMEM((pool, PAGE, 2 * HD), BF16),
            pltpu.VMEM((pool, PAGE, HD), BF16),
            pltpu.VMEM((width, units), BF16),
            pltpu.VMEM((width, units), BF16),
            pltpu.VMEM((units, width), BF16),
            pltpu.VMEM((pieces, heads * rows, 16 * PAGE), F32),
            pltpu.VMEM((NX, 2, 1, HD), F32),
            pltpu.VMEM((NX, nt, 1, HD), F32),
            pltpu.VMEM((rows, width), F32),
            pltpu.VMEM((ngrp, SLOT, width), BF16),
            pltpu.VMEM((2, nd, SLOT, width), BF16),
            pltpu.VMEM((nc, 2, hr, width), BF16),
            pltpu.VMEM((nc, nt, 2, hr, HD), BF16),
            pltpu.VMEM((nc, 2, hr, HD), BF16),
            pltpu.VMEM((nc, 6, 2, hr, HD), BF16),
            pltpu.VMEM((nc, nt, hr, HD), BF16),
            pltpu.VMEM((nc, 2, hr, width), BF16),
            pltpu.VMEM((nc, hr, width), BF16),
            pltpu.VMEM((nc, hr, width), BF16),
            pltpu.VMEM((nc, hr, width), BF16),
            pltpu.VMEM((2, nd, SLOT, width), BF16),
            pltpu.VMEM((2, nd, SLOT, width), BF16),
            pltpu.SemaphoreType.DMA((14,)),
            pltpu.SemaphoreType.DMA((copies,)),
            pltpu.SemaphoreType.DMA((copies,)),
        ],
        compiler_params=pltpu.CompilerParams(
            collective_id=0, has_side_effects=True, vmem_limit_bytes=60 * 1024 * 1024
        ),
    )(
        queries,
        new_keys,
        new_values,
        page_order,
        page_counts,
        residual,
        norm_gain,
        routes.T,
        route_weights.T,
        key_pages,
        value_pages,
        w_gate,
        w_up,
        w_down,
    )


def solution(mesh):
    sizes = (mesh.shape["attn"], mesh.shape["grp"], mesh.shape["tp"])

    def whole(*arrays):
        return jax.shard_map(
            functools.partial(local, sizes + (arrays[0].shape[1],)),
            mesh=mesh,
            in_specs=(
                P(("attn", "grp"), "tp"),
                P(("attn", "grp"), "tp"),
                P(("attn", "grp"), "tp"),
                P(("attn", "grp"), None, "tp"),
                P(("attn", "grp"), None, "tp"),
                P(("attn", "grp"), None),
                P(("attn", "grp"), None),
                P(("attn", "grp"), "tp"),
                P("tp"),
                P(("attn", "grp"), None),
                P(("attn", "grp"), None),
                P("grp", "tp", "attn"),
                P("grp", "tp", "attn"),
                P("grp", "attn", "tp"),
            ),
            out_specs=P(("attn", "grp"), "tp"),
            check_vma=False,
        )(*arrays)

    return whole
```

time: 106 us -> 78.2 us (0.74)
  Pallas kernels: 95.9 us -> 76.7 us
  local copies, waits for them, and re-layouts: 9.4 us -> 1.39 us
    pallas_call x1, Pallas kernels: 95.9 us -> 76.7 us  [local(): pl.pallas_call(functools.partial(kernel, sizes), out_shape=jax.ShapeDtype...]
    unnamed x27 -> x1, local copies, waits for them, and re-layouts: 8.66 us -> 1.39 us
where the time goes in v2:
time: 78.2 us; the launch traced here: 78.1 us
  Pallas kernels  76.7 us (98%)
  local copies, waits for them, and re-layouts  1.39 us (2%)
    pallas_call x1, Pallas kernels, local(): pl.pallas_call(functools.partial(kernel, sizes), out_shape=jax.ShapeDtype...  76.7 us

profile of v2, /device:TPU:1, one launch (start us, length us, event | category | flops | bytes accessed | tf_op | source)
XLA Modules:
  0.0 78.1 jit_solution(1241320523842300538)
XLA Ops:
  0.0 76.7 %shard_map.136 = bf16[24,768]{1,0:T(8,128)(2,1)} custom-call(bf16[24,768]{1,0:T(8,128)(2,1)} %q_hbm.1, bf16[24,128]{1,0:T(8,128)(2,1)} %nk_hbm.1, bf16[24,128]{1,0:T(8,128)(2,1)} %nv_hbm.1, s32[1,240]{1,0:T(1,128)} %order_hbm.1, s32[1,24]{1,0:T(1,128)} %counts_hbm.1, bf16[24,768]{1,0:T(8,128)(2,1)} %res_hbm.1, f32[768]{0:T(1024)} %gain_hbm.1, ...), custom_call_target="tpu_custom_call" | custom-call | tf_op jit(solution)/shard_map/pallas_call | solution.py:504
  76.7 1.4 %copy.16 = bf16[24,768]{1,0:T(8,128)(2,1)} copy(bf16[24,768]{1,0:T(8,128)(2,1)} %shard_map.136) | data formatting | bytes 73728

commit v3 on v2

--- a/solution.py
+++ b/solution.py
@@ -18,16 +18,18 @@
 NORM_EPSILON = 1e-05
 MASKED = -1e30
 MESH = pl.DeviceIdType.MESH
-IN, M1, RS2, SILU, AG2, M2, HOME, BACK = range(8)
+IN, M1, RS2, RS3, RS4, SILU, AG2, AG3, AG4, M2, HOME, BACK = range(12)
 ORDER = (
-    (IN, 0), (M1, 0), (IN, 7), (M1, 7), (IN, 2), (IN, 3), (RS2, 0), (IN, 1), (M1, 2), (IN, 5),
-    (M1, 1), (M1, 3), (IN, 4), (M1, 5), (IN, 6), (M1, 6), (M1, 4), (RS2, 3), (RS2, 5),
-    (RS2, 2), (RS2, 6), (RS2, 1), (SILU, 3), (RS2, 4), (SILU, 5), (SILU, 2), (SILU, 6),
-    (RS2, 7), (AG2, 3), (SILU, 1), (SILU, 4), (SILU, 0), (AG2, 6), (AG2, 5), (AG2, 2),
-    (SILU, 7), (M2, 3), (AG2, 1), (AG2, 4), (HOME, 3), (AG2, 0), (M2, 6), (M2, 5), (M2, 2),
-    (HOME, 6), (AG2, 7), (HOME, 2), (M2, 1), (HOME, 5), (M2, 4), (HOME, 1), (M2, 0), (HOME, 4),
+    (IN, 0), (M1, 0), (IN, 7), (IN, 1), (IN, 2), (M1, 7), (M1, 2), (M1, 1), (IN, 3), (IN, 4),
+    (M1, 3), (IN, 5), (M1, 4), (IN, 6), (M1, 6), (RS2, 2), (M1, 5), (RS2, 3), (RS2, 1),
+    (RS2, 4), (RS2, 5), (RS2, 6), (SILU, 2), (SILU, 3), (RS2, 0), (SILU, 1), (SILU, 5),
+    (SILU, 6), (RS2, 7), (AG2, 3), (SILU, 4), (AG2, 2), (AG2, 1), (AG2, 5), (AG2, 6),
+    (SILU, 0), (SILU, 7), (M2, 3), (AG2, 4), (M2, 2), (HOME, 3), (M2, 1), (HOME, 2), (M2, 5),
+    (M2, 6), (AG2, 0), (HOME, 1), (HOME, 5), (AG2, 7), (HOME, 6), (M2, 4), (HOME, 4), (M2, 0),
     (M2, 7), (BACK, 0), (BACK, 1),
 )
+SUM_BY_ONE = ()
+GATHER_BY_ONE = ()
 F32 = jnp.float32
 BF16 = jnp.bfloat16
 
@@ -343,14 +345,20 @@
                         h * hr : (h + 1) * hr, b * HD : (b + 1) * HD
                     ]
         far = block(4)
-        rs[c] = [
-            push(pre.at[c, far, 0], rs_half.at[c, 0], at_t(2)),
-            push(pre.at[c, far, 1], rs_half.at[c, 1], at_t(-2)),
-            push(pre.at[c, block(3)], rs_in.at[c, 0], at_t(1)),
-            push(pre.at[c, block(-3)], rs_in.at[c, 1], at_t(-1)),
-            push(pre.at[c, block(1)], rs_in.at[c, 2], at_t(1)),
-            push(pre.at[c, block(-1)], rs_in.at[c, 3], at_t(-1)),
-        ]
+        if c in SUM_BY_ONE:
+            rs[c] = [
+                push(pre.at[c, far, 0], rs_half.at[c, 0], at_t(1)),
+                push(pre.at[c, far, 1], rs_half.at[c, 1], at_t(-1)),
+            ]
+        else:
+            rs[c] = [
+                push(pre.at[c, far, 0], rs_half.at[c, 0], at_t(2)),
+                push(pre.at[c, far, 1], rs_half.at[c, 1], at_t(-2)),
+                push(pre.at[c, block(3)], rs_in.at[c, 0], at_t(1)),
+                push(pre.at[c, block(-3)], rs_in.at[c, 1], at_t(-1)),
+                push(pre.at[c, block(1)], rs_in.at[c, 2], at_t(1)),
+                push(pre.at[c, block(-1)], rs_in.at[c, 3], at_t(-1)),
+            ]
         dx, group = chunks[c]
         squares = jnp.sum(slots * slots, axis=1, keepdims=True)
         for h in range(2):
@@ -363,7 +371,31 @@
             ]
         seen.add(dx)
 
+    def task_rs_by_one(c, step):
+        out = []
+        for way, (here, to) in enumerate(((4 - step, 1), (step - 4, -1))):
+            rs[c][way].wait_recv()
+            here = block(here)
+            if step == 1:
+                pre[c, here, way] = (
+                    pre[c, here, way].astype(F32) + rs_half[c, way].astype(F32)
+                ).astype(BF16)
+            else:
+                pre[c, here] = (
+                    pre[c, here].astype(F32) + rs_in[c, 3 * way + step - 2].astype(F32)
+                ).astype(BF16)
+            out.append(push(pre.at[c, here], rs_in.at[c, 3 * way + step - 1], at_t(to)))
+        rs[c] = out
+
+    def task_rs3(c):
+        task_rs_by_one(c, 2)
+
+    def task_rs4(c):
+        task_rs_by_one(c, 3)
+
     def task_rs2(c):
+        if c in SUM_BY_ONE:
+            return task_rs_by_one(c, 1)
         out = []
         for way, (here, to) in enumerate(((block(2), at_t(2)), (block(-2), at_t(-2)))):
             rs[c][way].wait_recv()
@@ -388,14 +420,32 @@
         scale_row = lax.rsqrt(squares / width_all + NORM_EPSILON)
         scale = to_column(scale_row, hr, group * hr)
         total = pre[c, t].astype(F32)
-        for i in range(2, 6):
+        for i in (2, 5) if c in SUM_BY_ONE else range(2, 6):
             total = total + rs_in[c, i].astype(F32)
         gate, up = total[0] * scale, total[1] * scale
         act[c, t] = (gate / (1.0 + jnp.exp(-gate)) * up).astype(BF16)
         own = act.at[c, t]
-        ag[c] = [push(own, own, at_t(d)) for d in (2, -2, 1, -1)]
+        steps_y = (1, -1) if c in GATHER_BY_ONE else (2, -2, 1, -1)
+        ag[c] = [push(own, own, at_t(d)) for d in steps_y]
+
+    def task_ag_by_one(c, hop):
+        out = []
+        for way, d in enumerate((1, -1)):
+            ag[c][way].wait_recv()
+            if hop < 3 or way == c % 2:
+                arrived = act.at[c, block(-d * hop)]
+                out.append(push(arrived, arrived, at_t(d)))
+        ag[c] = out
+
+    def task_ag3(c):
+        task_ag_by_one(c, 2)
+
+    def task_ag4(c):
+        task_ag_by_one(c, 3)
 
     def task_ag2(c):
+        if c in GATHER_BY_ONE:
+            return task_ag_by_one(c, 1)
         out = []
         for way, d in enumerate((2, -2)):
             ag[c][way].wait_recv()
@@ -441,7 +491,20 @@
             else:
                 zback[group, i] = zsend[group, i]
 
-    tasks = (task_in, task_m1, task_rs2, task_silu, task_ag2, task_m2, task_home, task_back)
+    tasks = (
+        task_in,
+        task_m1,
+        task_rs2,
+        task_rs3,
+        task_rs4,
+        task_silu,
+        task_ag2,
+        task_ag3,
+        task_ag4,
+        task_m2,
+        task_home,
+        task_back,
+    )
     for i in range(11, 14):
         loads[i].wait()
     for task, c in ORDER:

time: 78.2 us -> 76.5 us (0.978)
  Pallas kernels: 76.7 us -> 74.2 us
    pallas_call x1, Pallas kernels: 76.7 us -> 74.2 us  [local(): pl.pallas_call(functools.partial(kernel, sizes), out_shape=jax.ShapeDtype...]
where the time goes in v3:
time: 76.5 us; the launch traced here: 75.6 us
  Pallas kernels  74.2 us (97%)
  local copies, waits for them, and re-layouts  1.39 us (2%)
    pallas_call x1, Pallas kernels, local(): pl.pallas_call(functools.partial(kernel, sizes), out_shape=jax.ShapeDtype...  74.2 us

profile of v3, /device:TPU:1, one launch (start us, length us, event | category | flops | bytes accessed | tf_op | source)
XLA Modules:
  0.0 75.6 jit_solution(16390031884778789668)
XLA Ops:
  0.0 74.2 %shard_map.136 = bf16[24,768]{1,0:T(8,128)(2,1)} custom-call(bf16[24,768]{1,0:T(8,128)(2,1)} %q_hbm.1, bf16[24,128]{1,0:T(8,128)(2,1)} %nk_hbm.1, bf16[24,128]{1,0:T(8,128)(2,1)} %nv_hbm.1, s32[1,240]{1,0:T(1,128)} %order_hbm.1, s32[1,24]{1,0:T(1,128)} %counts_hbm.1, bf16[24,768]{1,0:T(8,128)(2,1)} %res_hbm.1, f32[768]{0:T(1024)} %gain_hbm.1, ...), custom_call_target="tpu_custom_call" | custom-call | tf_op jit(solution)/shard_map/pallas_call | solution.py:567
  74.2 1.4 %copy.16 = bf16[24,768]{1,0:T(8,128)(2,1)} copy(bf16[24,768]{1,0:T(8,128)(2,1)} %shard_map.136) | data formatting | bytes 73728

commit v4 on v3

--- a/solution.py
+++ b/solution.py
@@ -174,7 +174,8 @@
     loads = []
     for i, (src, dst) in enumerate(pairs):
         loads.append(pltpu.make_async_copy(src, dst, local_sems.at[i]))
-        loads[i].start()
+        if i < 11:
+            loads[i].start()
 
     barrier = pltpu.get_barrier_semaphore()
     partners = [at_t(d) for d in range(1, nt)] + [sibling]
@@ -225,6 +226,8 @@
     own = jnp.sum(q_rows * new_key, axis=1, keepdims=True) * scale
 
     loads[4].wait()
+    for i in range(11, 14):
+        loads[i].start()
     pieces = scores.shape[0]
     pages = pool // pieces
     tokens = pages * PAGE
@@ -479,10 +482,10 @@
             c = index[dx, group]
             x_copy[c].wait_recv()
             total = total + xback[c].astype(F32)
-        spread = lax.dot_general(
-            pack, total.astype(BF16), (((0,), (0,)), ((), ())), preferred_element_type=F32
-        )
-        zsend[group] = spread.astype(BF16).reshape(nd, SLOT, width)
+        padding = jnp.zeros((SLOT - CAP, width), F32)
+        for i in range(nd):
+            piece = [total[i * CAP : (i + 1) * CAP], padding]
+            zsend[group, i] = jnp.concatenate(piece, axis=0).astype(BF16)
         for i, d in enumerate(groups[group]):
             if d:
                 home[group, i] = push(

time: 76.5 us -> 76.3 us (level)
  no operation moved by 1% of the time
where the time goes in v4:
time: 76.3 us; the launch traced here: 75.5 us
  Pallas kernels  74.1 us (97%)
  local copies, waits for them, and re-layouts  1.39 us (2%)
    pallas_call x1, Pallas kernels, local(): pl.pallas_call(functools.partial(kernel, sizes), out_shape=jax.ShapeDtype...  74.1 us

profile of v4, /device:TPU:1, one launch (start us, length us, event | category | flops | bytes accessed | tf_op | source)
XLA Modules:
  0.0 75.5 jit_solution(9195957166550538373)
XLA Ops:
  0.0 74.1 %shard_map.136 = bf16[24,768]{1,0:T(8,128)(2,1)} custom-call(bf16[24,768]{1,0:T(8,128)(2,1)} %q_hbm.1, bf16[24,128]{1,0:T(8,128)(2,1)} %nk_hbm.1, bf16[24,128]{1,0:T(8,128)(2,1)} %nv_hbm.1, s32[1,240]{1,0:T(1,128)} %order_hbm.1, s32[1,24]{1,0:T(1,128)} %counts_hbm.1, bf16[24,768]{1,0:T(8,128)(2,1)} %res_hbm.1, f32[768]{0:T(1024)} %gain_hbm.1, ...), custom_call_target="tpu_custom_call" | custom-call | tf_op jit(solution)/shard_map/pallas_call | solution.py:570
  74.1 1.4 %copy.16 = bf16[24,768]{1,0:T(8,128)(2,1)} copy(bf16[24,768]{1,0:T(8,128)(2,1)} %shard_map.136) | data formatting | bytes 73728
